TPU v7x, 32 devices: a whole 2x2x4 slice. The times are simulated.
32 devices in a mesh: groups: 2 (over x), vocab: 16 (over z, y, core).
Axes of the slice: x: 2, y: 2, z: 4, core: 2. Of those that a mesh axis runs over, the one named last changes fastest.
Arguments:
- hidden: bfloat16 [8192, 3584], P(('groups', 'vocab')), parts along dimension 0, may hold values from -6 to 6
- head_weight: bfloat16 [76032, 3584], P('vocab'), may hold values from -0.29882812 to 0.29882812
- term_grad: float32 [32, 76032], P('groups', 'vocab'), parts along dimension 0, may hold values from -24 to 24
- winner: int32 [32, 76032], P('groups', 'vocab'), parts along dimension 0, may hold values from 0 to 63
- route: int32 [2048, 2], P(('groups', 'vocab')), parts along dimension 0, may hold values from 0 to 15, all different within a row; in each aligned block of 64 rows (0 to 63, 64 to 127, ...) at most 16 rows name the same one
Outputs:
- weight_grad: bfloat16 [152064, 3584], P(('groups', 'vocab')), parts along dimension 0
- hidden_grad: bfloat16 [8192, 3584], P(('groups', 'vocab')), parts along dimension 0
There are 2 independent parts, one for each index of `groups`. A program takes and returns all parts, laid end to end along the dimension named above; an argument that names none is the same for every part. Nothing has to cross between parts.
Inputs may be any that keep to these rules, and one draw needn't show every extreme that they name: `winner`: A code is a slot c of the document's blocks listed for the entry's tile times 4 plus a position in that block; codes whose slot is not filled name no token. `route`: each block names 2 different tiles; among the blocks of one document at most 16 name the same tile, and in every draw some tile is named by exactly 16 blocks of some document.
All inputs are finite; a program needn't handle non-finite values.
Results may differ from a plain program's by a relative error of at most 0.0059.
Values may be sent and summed in bfloat16 or wider, within the bound.
A program may use at most 256 MiB of HBM per device.

v0:
```python
import functools

import jax
import jax.numpy as jnp
from jax import lax
from jax.experimental import pallas as pl
from jax.experimental.pallas import tpu as pltpu
from jax.sharding import PartitionSpec as P

BLOCK = 4
V_TILE = 512
OUT_CHUNKS = 2
BACK_CHUNKS = 2
PAIRED_MOST = 8
VMEM = 56 * 1024 * 1024


def saturation_slope(x):
    small = jnp.exp(-jnp.abs(x))
    softplus = jnp.maximum(x, 0.0) + jnp.log1p(small)
    sigmoid = jnp.where(x >= 0, 1.0, small) / (1.0 + small)
    return sigmoid / (1.0 + softplus)


def delta_kernel(docs, x_ref, w_ref, winner_ref, grad_ref, delta_ref):
    rows, width = delta_ref.shape
    logits = lax.dot_general(
        x_ref[...], w_ref[...], (((1,), (1,)), ((), ())), preferred_element_type=jnp.float32
    )
    logits = logits.reshape(docs, rows // docs, width)
    codes = lax.broadcasted_iota(jnp.int32, logits.shape, 1)
    chosen = winner_ref[...][:, None, :] == codes
    picked = jnp.sum(jnp.where(chosen, logits, 0.0), axis=1)
    delta = grad_ref[...] * saturation_slope(picked)
    spread = jnp.where(chosen, delta[:, None, :], 0.0)
    delta_ref[...] = spread.reshape(rows, width).astype(jnp.bfloat16)


def term_deltas(rows, weight, winner, grad):
    count, width = rows.shape
    vocab = weight.shape[0]
    docs = winner.shape[0]
    return pl.pallas_call(
        functools.partial(delta_kernel, docs),
        grid=(pl.cdiv(vocab, V_TILE),),
        in_specs=[
            pl.BlockSpec((count, width), lambda i: (0, 0)),
            pl.BlockSpec((V_TILE, width), lambda i: (i, 0)),
            pl.BlockSpec((docs, V_TILE), lambda i: (0, i)),
            pl.BlockSpec((docs, V_TILE), lambda i: (0, i)),
        ],
        out_specs=pl.BlockSpec((count, V_TILE), lambda i: (0, i)),
        out_shape=jax.ShapeDtypeStruct((count, vocab), jnp.bfloat16),
        compiler_params=pltpu.CompilerParams(vmem_limit_bytes=VMEM),
        cost_estimate=pl.CostEstimate(
            flops=2 * count * vocab * width,
            bytes_accessed=2 * vocab * width + 2 * count * (vocab + width),
            transcendentals=0,
        ),
        name="term_deltas",
    )(rows, weight, winner, grad)


def weight_kernel(da_ref, db_ref, xa_ref, xb_ref, out_ref):
    dims = (((0,), (0,)), ((), ()))
    total = lax.dot_general(da_ref[...], xa_ref[...], dims, preferred_element_type=jnp.float32)
    total += lax.dot_general(db_ref[...], xb_ref[...], dims, preferred_element_type=jnp.float32)
    out_ref[...] = total.astype(jnp.bfloat16)


def weight_grads(delta_a, delta_b, rows_a, rows_b):
    count, vocab = delta_a.shape
    width = rows_a.shape[1]
    whole = pl.BlockSpec((count, width), lambda i: (0, 0))
    part = pl.BlockSpec((count, V_TILE), lambda i: (0, i))
    return pl.pallas_call(
        weight_kernel,
        grid=(pl.cdiv(vocab, V_TILE),),
        in_specs=[part, part, whole, whole],
        out_specs=pl.BlockSpec((V_TILE, width), lambda i: (i, 0)),
        out_shape=jax.ShapeDtypeStruct((vocab, width), jnp.bfloat16),
        compiler_params=pltpu.CompilerParams(vmem_limit_bytes=VMEM),
        cost_estimate=pl.CostEstimate(
            flops=4 * count * vocab * width,
            bytes_accessed=2 * vocab * width + 4 * count * (vocab + width),
            transcendentals=0,
        ),
        name="weight_grads",
    )(delta_a, delta_b, rows_a, rows_b)


TILE = 256
RELAY_CHUNKS = 2
BACK_WIDTH = 512
MESH = pl.DeviceIdType.MESH


def fused_kernel(
    hidden, near_pick, far_pick, winner, grad, weight,
    weight_grad, hidden_grad,
    relay, near_out, far_out, rows, delta, w_tiles, w_columns, g_tiles, landing, back_out, back_in,
    relay_send, relay_recv, near_send, near_recv, far_send, far_recv,
    home_send, home_recv, part_send, part_recv, back_send, back_recv, tile_sem, column_sem, grad_sem,
):
    tokens, width = hidden.shape
    vocab = weight.shape[0]
    tiles, docs, _ = winner.shape
    near_docs = docs // 2
    count = near_out.shape[0]
    slot = count // near_docs
    peers = near_docs
    me = lax.axis_index("vocab")
    side = me // peers
    local = me % peers
    across = (me + peers) % (2 * peers)
    overlap = tiles * TILE - vocab

    def peer(k):
        flipped, scale = 0, 1
        while scale < peers:
            bit = local // scale % 2
            flipped = flipped + scale * ((1 - bit) if k & scale else bit)
            scale *= 2
        return side * peers + flipped

    def send(src, dst, send_sem, recv_sem, device):
        return pltpu.make_async_remote_copy(
            src_ref=src, dst_ref=dst, send_sem=send_sem, recv_sem=recv_sem,
            device_id={"vocab": device}, device_id_type=MESH,
        )

    def slots(k):
        return pl.ds(k * slot, slot)

    barrier = pltpu.get_barrier_semaphore()
    for k in range(1, peers):
        pl.semaphore_signal(barrier, inc=1, device_id={"vocab": peer(k)}, device_id_type=MESH)
    pl.semaphore_signal(barrier, inc=1, device_id={"vocab": across}, device_id_type=MESH)
    pl.semaphore_wait(barrier, peers)

    relay_width = width // RELAY_CHUNKS
    relays = []
    for c in range(RELAY_CHUNKS):
        part = pl.ds(c * relay_width, relay_width)
        relays.append(
            send(hidden.at[:, part], relay.at[:, part], relay_send.at[c], relay_recv.at[c], across)
        )
        relays[c].start()

    def tile_copy(i, place):
        start = pl.multiple_of(i * TILE - i // (tiles - 1) * overlap, 16)
        return pltpu.make_async_copy(
            weight.at[pl.ds(start, TILE), :], w_tiles.at[place], tile_sem.at[place]
        )

    def column_copies(j, place):
        columns = pl.ds(pl.multiple_of(j * TILE, TILE), TILE)
        full = (tiles - 1) * TILE
        return (
            pltpu.make_async_copy(
                weight.at[pl.ds(0, full), columns],
                w_columns.at[place, pl.ds(0, full), :],
                column_sem.at[place, 0],
            ),
            pltpu.make_async_copy(
                weight.at[pl.ds(vocab - TILE, TILE), columns],
                w_columns.at[place, pl.ds(full, TILE), :],
                column_sem.at[place, 1],
            ),
        )

    def start_columns(j, place):
        for copy in column_copies(j, place):
            copy.start()

    near_out[...] = jnp.dot(
        near_pick[...], hidden[...], preferred_element_type=jnp.float32
    ).astype(jnp.bfloat16)
    near_sends = []
    for k in range(1, peers):
        copy = send(
            near_out.at[slots(k), :], rows.at[slots(k), :], near_send.at[k], near_recv.at[k], peer(k)
        )
        copy.start()
        near_sends.append(copy)
    rows[pl.ds(0, slot), :] = near_out[pl.ds(0, slot), :]

    far_sends = []

    def pass_on(c):
        relays[c].wait_recv()
        part = pl.ds(c * relay_width, relay_width)
        far_out[:, part] = jnp.dot(
            far_pick[...], relay[:, part], preferred_element_type=jnp.float32
        ).astype(jnp.bfloat16)
        for k in range(1, peers):
            copy = send(
                far_out.at[slots(k), part],
                rows.at[pl.ds(count + k * slot, slot), part],
                far_send.at[c, k],
                far_recv.at[c, k],
                peer(k),
            )
            copy.start()
            far_sends.append(copy)
        rows[pl.ds(count, slot), part] = far_out[pl.ds(0, slot), part]

    def deltas(row, doc):
        tile_copy(0, 0).start()

        def body(i, carry):
            place = i % 2

            @pl.when(i + 1 < tiles)
            def _():
                tile_copy(i + 1, 1 - place).start()

            tile_copy(i, place).wait()
            logits = lax.dot_general(
                rows[pl.ds(row, count), :],
                w_tiles[place],
                (((1,), (1,)), ((), ())),
                preferred_element_type=jnp.float32,
            )
            logits = logits.reshape(near_docs, slot, TILE)
            codes = lax.broadcasted_iota(jnp.int32, logits.shape, 1)
            chosen = winner[i, pl.ds(doc, near_docs), :][:, None, :] == codes
            picked = jnp.sum(jnp.where(chosen, logits, 0.0), axis=1)
            term = grad[i, pl.ds(doc, near_docs), :] * saturation_slope(picked)
            spread = jnp.where(chosen, term[:, None, :], 0.0)
            delta[pl.ds(row, count), pl.ds(pl.multiple_of(i * TILE, TILE), TILE)] = spread.reshape(
                count, TILE
            ).astype(jnp.bfloat16)
            return carry

        lax.fori_loop(0, tiles, body, 0)

    columns = width // TILE

    def column_step(row, j, out, home):
        place = j % 2

        @pl.when(j + 1 < columns)
        def _():
            start_columns(j + 1, 1 - place)

        for copy in column_copies(j, place):
            copy.wait()
        value = jnp.dot(
            delta[pl.ds(row, count), :], w_columns[place], preferred_element_type=jnp.float32
        ).astype(jnp.bfloat16)
        where = pl.ds(pl.multiple_of(j * TILE, TILE), TILE)
        out[:, where] = value
        landing[home, pl.ds(0, slot), where] = value[:slot]

    pass_on(0)
    for copy in near_sends:
        copy.wait_recv()
    start_columns(0, 0)
    deltas(0, 0)
    for c in range(1, RELAY_CHUNKS):
        pass_on(c)
    for copy in near_sends:
        copy.wait_send()

    def near_column(j, carry):
        column_step(0, j, near_out, 0)
        return carry

    lax.fori_loop(0, columns, near_column, 0)
    start_columns(0, 0)
    for copy in far_sends:
        copy.wait_recv()
    homes = []
    for k in range(1, peers):
        copy = send(
            near_out.at[slots(k), :],
            landing.at[0, slots(k), :],
            home_send.at[k],
            home_recv.at[k],
            peer(k),
        )
        copy.start()
        homes.append(copy)
    deltas(count, near_docs)
    for copy in far_sends:
        copy.wait_send()
    per_chunk = BACK_WIDTH // TILE
    chunks = width // BACK_WIDTH

    def part_copy(c, k):
        part = pl.ds(pl.multiple_of(c * BACK_WIDTH, BACK_WIDTH), BACK_WIDTH)
        return send(
            far_out.at[slots(k), part],
            landing.at[1, slots(k), part],
            part_send.at[c, k],
            part_recv.at[c, k],
            peer(k),
        )

    def far_columns(c, carry):
        for t in range(per_chunk):
            column_step(count, c * per_chunk + t, far_out, 1)
        for k in range(1, peers):
            part_copy(c, k).start()
        return carry

    lax.fori_loop(0, chunks, far_columns, 0)

    def back_copy(c):
        part = pl.ds(pl.multiple_of(c * BACK_WIDTH, BACK_WIDTH), BACK_WIDTH)
        return send(
            back_out.at[:, part], back_in.at[:, part], back_send.at[c], back_recv.at[c], across
        )

    gather = (((0,), (0,)), ((), ()))

    def pass_back(c):
        for k in range(1, peers):
            part_copy(c, k).wait()
        part = pl.ds(pl.multiple_of(c * BACK_WIDTH, BACK_WIDTH), BACK_WIDTH)
        back_out[:, part] = lax.dot_general(
            far_pick[...], landing[1, :, part], gather, preferred_element_type=jnp.float32
        ).astype(jnp.bfloat16)
        back_copy(c).start()

    def grad_copy(i, place):
        start = pl.multiple_of(i * TILE, TILE)
        return pltpu.make_async_copy(
            g_tiles.at[place], weight_grad.at[pl.ds(start, TILE), :], grad_sem.at[place]
        )

    def grad_tile(i):
        return lax.dot_general(
            delta[:, pl.ds(pl.multiple_of(i * TILE, TILE), TILE)],
            rows[...],
            gather,
            preferred_element_type=jnp.float32,
        ).astype(jnp.bfloat16)

    def grad_body(i, carry):
        place = i % 2

        @pl.when(i >= 2)
        def _():
            grad_copy(i - 2, place).wait()

        g_tiles[place] = grad_tile(i)
        grad_copy(i, place).start()

        @pl.when((i % 2 == 1) & (i // 2 < chunks))
        def _():
            pass_back(i // 2)

        return carry

    lax.fori_loop(0, tiles - 1, grad_body, 0)
    last = tiles - 1
    grad_copy(last - 2, last % 2).wait()
    g_tiles[last % 2] = grad_tile(last)
    tail = pltpu.make_async_copy(
        g_tiles.at[last % 2, pl.ds(overlap, TILE - overlap), :],
        weight_grad.at[pl.ds(last * TILE, TILE - overlap), :],
        grad_sem.at[last % 2],
    )
    tail.start()
    for copy in homes:
        copy.wait()

    def finish(c, carry):
        back_copy(c).wait()
        part = pl.ds(pl.multiple_of(c * BACK_WIDTH, BACK_WIDTH), BACK_WIDTH)
        own = lax.dot_general(
            near_pick[...], landing[0, :, part], gather, preferred_element_type=jnp.float32
        )
        hidden_grad[:, part] = (own + back_in[:, part].astype(jnp.float32)).astype(jnp.bfloat16)
        return carry

    lax.fori_loop(0, chunks, finish, 0)
    for copy in relays:
        copy.wait_send()
    grad_copy(last - 1, (last - 1) % 2).wait()
    tail.wait()


def fused(hidden, near_pick, far_pick, winner, grad, weight):
    tokens, width = hidden.shape
    vocab = weight.shape[0]
    count = near_pick.shape[0]
    tiles, docs, _ = winner.shape
    peers = docs // 2
    chunks = width // BACK_WIDTH
    held = jnp.bfloat16
    dma = pltpu.SemaphoreType.DMA
    vmem = pl.BlockSpec(memory_space=pltpu.VMEM)
    hbm = pl.BlockSpec(memory_space=pl.ANY)
    return pl.pallas_call(
        fused_kernel,
        in_specs=[vmem] * 5 + [hbm],
        out_specs=[hbm, vmem],
        out_shape=[
            jax.ShapeDtypeStruct((vocab, width), held),
            jax.ShapeDtypeStruct((tokens, width), held),
        ],
        scratch_shapes=[
            pltpu.VMEM((tokens, width), held),
            pltpu.VMEM((count, width), held),
            pltpu.VMEM((count, width), held),
            pltpu.VMEM((2 * count, width), held),
            pltpu.VMEM((2 * count, tiles * TILE), held),
            pltpu.VMEM((2, TILE, width), held),
            pltpu.VMEM((2, tiles * TILE, TILE), held),
            pltpu.VMEM((2, TILE, width), held),
            pltpu.VMEM((2, count, width), held),
            pltpu.VMEM((tokens, width), held),
            pltpu.VMEM((tokens, width), held),
            dma((RELAY_CHUNKS,)), dma((RELAY_CHUNKS,)),
            dma((peers,)), dma((peers,)),
            dma((RELAY_CHUNKS, peers)), dma((RELAY_CHUNKS, peers)),
            dma((peers,)), dma((peers,)),
            dma((chunks, peers)), dma((chunks, peers)),
            dma((chunks,)), dma((chunks,)),
            dma((2,)), dma((2, 2)), dma((2,)),
        ],
        compiler_params=pltpu.CompilerParams(
            collective_id=0, has_side_effects=True, vmem_limit_bytes=62 * 1024 * 1024
        ),
        name="fused",
    )(hidden, near_pick, far_pick, winner, grad, weight)


def tiled(x, blank):
    vocab = x.shape[1]
    tiles = pl.cdiv(vocab, TILE)
    full = (tiles - 1) * TILE
    tail = x[:, vocab - TILE :]
    if blank:
        fresh = jnp.arange(TILE) >= tiles * TILE - vocab
        tail = jnp.where(fresh[None, :], tail, 0)
    whole = jnp.concatenate([x[:, :full], tail], axis=1)
    return whole.reshape(x.shape[0], tiles, TILE).swapaxes(0, 1)


def on_device(hidden, head_weight, term_grad, winner, route):
    n = lax.axis_size("vocab")
    half = n // 2
    me = lax.axis_index("vocab")
    tokens, width = hidden.shape
    block_count = route.shape[0]
    capacity = 2 * max(1, block_count * route.shape[1] // n)
    slot_rows = capacity * BLOCK
    base = me // half * half
    peers = jnp.arange(half, dtype=jnp.int32)
    paired = half <= PAIRED_MOST and half & (half - 1) == 0
    if paired:
        peers = peers ^ (me % half)
    near, far = base + peers, (half - base) + peers

    def cross(x):
        return lax.ppermute(x, "vocab", [(i, (i + half) % n) for i in range(n)])

    def exchange(pieces):
        if not paired:
            sides = [list(range(half)), list(range(half, n))]
            return list(lax.all_to_all(pieces, "vocab", 0, 0, axis_index_groups=sides, tiled=True))
        pieces = list(pieces)
        return [pieces[0]] + [
            lax.ppermute(pieces[k], "vocab", [(i, i ^ k) for i in range(n)])
            for k in range(1, half)
        ]

    def chooser(table):
        listed = jnp.any(table[:, :, None] == near[None, None, :], axis=1)
        ranking = jnp.cumsum(listed.astype(jnp.int32), axis=0) - 1
        slot = jnp.where(listed, ranking, -1)
        slots = jnp.arange(half * slot_rows, dtype=jnp.int32)
        place = jnp.arange(tokens, dtype=jnp.int32)
        wanted = jnp.repeat(jnp.repeat(slot.T, BLOCK, axis=1), slot_rows, axis=0)
        match = wanted == (slots % slot_rows // BLOCK)[:, None]
        match &= (slots % BLOCK)[:, None] == (place % BLOCK)[None, :]
        return match.astype(jnp.bfloat16)

    def select(pick, rows):
        chosen = jnp.dot(pick, rows, preferred_element_type=jnp.float32).astype(jnp.bfloat16)
        return chosen.reshape(half, slot_rows, rows.shape[1])

    def gather_back(pick, parts):
        return lax.dot_general(
            pick,
            jnp.concatenate(parts, axis=0),
            (((0,), (0,)), ((), ())),
            preferred_element_type=jnp.float32,
        )

    out_step = width // OUT_CHUNKS
    back_step = width // BACK_CHUNKS
    far_route = cross(route)
    near_pick, far_pick = chooser(route), chooser(far_route)
    if paired and slot_rows % 16 == 0:
        order = jnp.concatenate([near, far])
        return tuple(
            fused(
                hidden,
                near_pick,
                far_pick,
                tiled(winner[order], False),
                tiled(term_grad[order], True),
                head_weight,
            )
        )
    far_hidden = [cross(hidden[:, c * out_step : (c + 1) * out_step]) for c in range(OUT_CHUNKS)]
    near_rows = jnp.concatenate(exchange(select(near_pick, hidden)), axis=0)
    far_rows = [
        jnp.concatenate(exchange(select(far_pick, piece)), axis=0) for piece in far_hidden
    ]
    far_rows = jnp.concatenate(far_rows, axis=1)

    near_delta = term_deltas(near_rows, head_weight, winner[near], term_grad[near])
    far_delta = term_deltas(far_rows, head_weight, winner[far], term_grad[far])

    def parts(delta, c):
        value = jnp.dot(
            delta,
            head_weight[:, c * back_step : (c + 1) * back_step],
            preferred_element_type=jnp.float32,
        ).astype(jnp.bfloat16)
        return exchange(value.reshape(half, slot_rows, back_step))

    far_sum = [
        cross(gather_back(far_pick, parts(far_delta, c)).astype(jnp.bfloat16))
        for c in range(BACK_CHUNKS)
    ]
    near_sum = [gather_back(near_pick, parts(near_delta, c)) for c in range(BACK_CHUNKS)]
    hidden_grad = jnp.concatenate(
        [
            (a + b.astype(jnp.float32)).astype(jnp.bfloat16)
            for a, b in zip(near_sum, far_sum)
        ],
        axis=1,
    )
    weight_grad = weight_grads(near_delta, far_delta, near_rows, far_rows)
    return (weight_grad, hidden_grad)


def solution(mesh):
    placed = (
        P(("groups", "vocab"), None),
        P("vocab", None),
        P("groups", "vocab"),
        P("groups", "vocab"),
        P(("groups", "vocab"), None),
    )
    return jax.shard_map(
        on_device,
        mesh=mesh,
        in_specs=placed,
        out_specs=(P(("groups", "vocab"), None), P(("groups", "vocab"), None)),
        check_vma=False,
    )
```

profile of v0, /device:TPU:1, one launch (start us, length us, event | category | flops | bytes accessed | tf_op | source)
XLA Modules:
  0.0 327.3 jit_solution(2852848506495344983)
XLA Ops:
  0.6 0.0 copy-start
  0.6 3.2 collective-permute-start
  3.9 0.1 fusion.11
  4.0 0.0 copy-done
  4.0 0.7 gather_fusion
  4.7 0.1 slice.21
  4.8 1.8 gather_fusion.1
  6.6 0.1 slice_select_fusion
  6.7 0.8 copy.29
  7.5 0.8 copy.30
  8.2 0.0 collective-permute-done
  8.2 0.8 compare_reduce_fusion
  9.0 0.1 copy.18
  9.1 0.1 copy.21
  9.2 0.1 copy.17
  9.3 0.1 reduce_window_sum.17
  9.4 0.1 copy.20
  9.5 0.1 reduce_window_sum.18
  9.6 0.1 copy.22
  9.7 0.1 copy.19
  9.8 1.1 fusion.1
  10.8 291.3 %fused.1 = (bf16[4752,3584]{1,0:T(8,128)(2,1)}, bf16[256,3584]{1,0:T(8,128)(2,1)}) custom-call(bf16[256,3584]{1,0:T(8,128)(2,1)} %hidden.1, bf16[512,256]{1,0:T(8,128)(2,1)} %get-tuple-element.5.near_pick, bf16[512,256]{1,0:T(8,128)(2,1)} %get-tuple-element.4.far_pick, s32[19,16,256]{2,1,0:T(8,128)} %bitcast.39, f32[19,16,256]{2,1,0:T(8,128)} %bitcast.38, ...), custom_call_target="tpu_custom_call" | custom-call | tf_op jit(solution)/shard_map/fused/pallas_call | solution.py:397
  302.2 0.0 copy-start.1
  302.2 0.0 copy-start.2
  302.2 23.9 %copy.33 = bf16[4752,3584]{1,0:T(8,128)(2,1)} copy(bf16[4752,3584]{1,0:T(8,128)(2,1)} %get-tuple-element.10) | data formatting | bytes 68124672
  326.1 0.0 copy-done.2
  326.1 1.2 copy.34
  327.3 0.0 copy-done.1
  (17 shorter events, 0.2 us)
Async XLA Ops:
  0.6 3.4 %copy-start = (s32[16,4752]{1,0:T(8,128)S(1)}, s32[16,4752]{1,0:T(8,128)}, u32[]{:S(2)}) copy-start(s32[16,4752]{1,0:T(8,128)} %param.8) | copy-start | bytes 912388
  0.6 7.6 %collective-permute-start = (s32[64,2]{0,1:T(2,128)}, s32[64,2]{0,1:T(2,128)S(1)}, u32[]{:S(2)}, u32[]{:S(2)}) collective-permute-start(s32[64,2]{0,1:T(2,128)} %param.9), channel_id=1, source_target_pairs={{0,8},{1,9},{2,10},{3,11},{4,12},{5,13},{6,14},{7,15},{8,0},{9,1},... | collective-permute-start | bytes 1544 | tf_op jit(solution)/shard_map/ppermute | solution.py:460
  302.2 25.1 %copy-start.1 = (s32[16,4752]{1,0:T(8,128)S(1)}, s32[16,4752]{1,0:T(8,128)}, u32[]{:S(2)}) copy-start(s32[16,4752]{1,0:T(8,128)} %param.8) | copy-start | bytes 912388
  302.2 23.9 %copy-start.2 = (bf16[256,3584]{1,0:T(8,128)(2,1)S(1)}, bf16[256,3584]{1,0:T(8,128)(2,1)}, u32[]{:S(2)}) copy-start(bf16[256,3584]{1,0:T(8,128)(2,1)} %get-tuple-element.11) | copy-start | bytes 5505028
where the time goes:
time: 329 us; the launch traced here: 327 us
  Pallas kernels  291 us (88%)
  local copies, waits for them, and re-layouts  29.7 us (9%)
    pallas_call x1, Pallas kernels, fused(): pl.pallas_call(fused_kernel, in_specs=[vmem] * 5 + [hbm], out_specs=[hbm,...  291 us
    unnamed x8, local copies, waits for them, and re-layouts  25.1 us
  transfers between devices with their start and end apart: 1, of which 0 were waited for; matrix products, arithmetic and copies ran while one was open for 1% of the time, Pallas kernels for 0%

commit v1 on v0

--- a/solution.py
+++ b/solution.py
@@ -8,6 +8,7 @@
 from jax.sharding import PartitionSpec as P
 
 BLOCK = 4
+TOP = 2
 V_TILE = 512
 OUT_CHUNKS = 2
 BACK_CHUNKS = 2
@@ -96,10 +97,11 @@
 
 
 def fused_kernel(
-    hidden, near_pick, far_pick, winner, grad, weight,
+    hidden, route, winner, grad, weight,
     weight_grad, hidden_grad,
+    near_pick, far_pick, far_route,
     relay, near_out, far_out, rows, delta, w_tiles, w_columns, g_tiles, landing, back_out, back_in,
-    relay_send, relay_recv, near_send, near_recv, far_send, far_recv,
+    route_send, route_recv, relay_send, relay_recv, near_send, near_recv, far_send, far_recv,
     home_send, home_recv, part_send, part_recv, back_send, back_recv, tile_sem, column_sem, grad_sem,
 ):
     tokens, width = hidden.shape
@@ -138,6 +140,8 @@
     pl.semaphore_signal(barrier, inc=1, device_id={"vocab": across}, device_id_type=MESH)
     pl.semaphore_wait(barrier, peers)
 
+    route_copy = send(route, far_route, route_send, route_recv, across)
+    route_copy.start()
     relay_width = width // RELAY_CHUNKS
     relays = []
     for c in range(RELAY_CHUNKS):
@@ -173,6 +177,28 @@
         for copy in column_copies(j, place):
             copy.start()
 
+    def chooser(table):
+        tile = lax.broadcasted_iota(jnp.int32, (peers, tokens), 0)
+        tile = side * peers + (tile ^ local)
+        listed = jnp.zeros((peers, tokens), jnp.bool_)
+        for t in range(TOP):
+            listed |= table[t : t + 1, :] == tile
+        above = lax.broadcasted_iota(jnp.int32, (tokens, tokens), 0)
+        below = lax.broadcasted_iota(jnp.int32, (tokens, tokens), 1)
+        earlier = (above % BLOCK == 0) & (above // BLOCK < below // BLOCK)
+        ranking = jnp.dot(
+            jnp.where(listed, 1.0, 0.0).astype(jnp.bfloat16),
+            jnp.where(earlier, 1.0, 0.0).astype(jnp.bfloat16),
+            preferred_element_type=jnp.float32,
+        ).astype(jnp.int32)
+        place = jnp.where(listed, ranking, -1)
+        shape = (peers, slot, tokens)
+        entry = lax.broadcasted_iota(jnp.int32, shape, 1)
+        token = lax.broadcasted_iota(jnp.int32, shape, 2)
+        match = (place[:, None, :] == entry // BLOCK) & (entry % BLOCK == token % BLOCK)
+        return jnp.where(match, 1.0, 0.0).reshape(count, tokens).astype(jnp.bfloat16)
+
+    near_pick[...] = chooser(route[...])
     near_out[...] = jnp.dot(
         near_pick[...], hidden[...], preferred_element_type=jnp.float32
     ).astype(jnp.bfloat16)
@@ -253,6 +279,8 @@
         out[:, where] = value
         landing[home, pl.ds(0, slot), where] = value[:slot]
 
+    route_copy.wait_recv()
+    far_pick[...] = chooser(far_route[...])
     pass_on(0)
     for copy in near_sends:
         copy.wait_recv()
@@ -377,18 +405,19 @@
         return carry
 
     lax.fori_loop(0, chunks, finish, 0)
+    route_copy.wait_send()
     for copy in relays:
         copy.wait_send()
     grad_copy(last - 1, (last - 1) % 2).wait()
     tail.wait()
 
 
-def fused(hidden, near_pick, far_pick, winner, grad, weight):
+def fused(hidden, route, winner, grad, weight, slot_rows):
     tokens, width = hidden.shape
     vocab = weight.shape[0]
-    count = near_pick.shape[0]
     tiles, docs, _ = winner.shape
     peers = docs // 2
+    count = peers * slot_rows
     chunks = width // BACK_WIDTH
     held = jnp.bfloat16
     dma = pltpu.SemaphoreType.DMA
@@ -396,13 +425,16 @@
     hbm = pl.BlockSpec(memory_space=pl.ANY)
     return pl.pallas_call(
         fused_kernel,
-        in_specs=[vmem] * 5 + [hbm],
+        in_specs=[vmem] * 4 + [hbm],
         out_specs=[hbm, vmem],
         out_shape=[
             jax.ShapeDtypeStruct((vocab, width), held),
             jax.ShapeDtypeStruct((tokens, width), held),
         ],
         scratch_shapes=[
+            pltpu.VMEM((count, tokens), held),
+            pltpu.VMEM((count, tokens), held),
+            pltpu.VMEM(route.shape, jnp.int32),
             pltpu.VMEM((tokens, width), held),
             pltpu.VMEM((count, width), held),
             pltpu.VMEM((count, width), held),
@@ -414,6 +446,7 @@
             pltpu.VMEM((2, count, width), held),
             pltpu.VMEM((tokens, width), held),
             pltpu.VMEM((tokens, width), held),
+            dma, dma,
             dma((RELAY_CHUNKS,)), dma((RELAY_CHUNKS,)),
             dma((peers,)), dma((peers,)),
             dma((RELAY_CHUNKS, peers)), dma((RELAY_CHUNKS, peers)),
@@ -426,7 +459,7 @@
             collective_id=0, has_side_effects=True, vmem_limit_bytes=62 * 1024 * 1024
         ),
         name="fused",
-    )(hidden, near_pick, far_pick, winner, grad, weight)
+    )(hidden, route, winner, grad, weight)
 
 
 def tiled(x, blank):
@@ -494,20 +527,22 @@
 
     out_step = width // OUT_CHUNKS
     back_step = width // BACK_CHUNKS
-    far_route = cross(route)
-    near_pick, far_pick = chooser(route), chooser(far_route)
     if paired and slot_rows % 16 == 0:
         order = jnp.concatenate([near, far])
+        listing = jnp.repeat(route.T, BLOCK, axis=1)
+        listing = jnp.pad(listing, ((0, -route.shape[1] % 8), (0, 0)), constant_values=-1)
         return tuple(
             fused(
                 hidden,
-                near_pick,
-                far_pick,
+                listing,
                 tiled(winner[order], False),
                 tiled(term_grad[order], True),
                 head_weight,
+                slot_rows,
             )
         )
+    far_route = cross(route)
+    near_pick, far_pick = chooser(route), chooser(far_route)
     far_hidden = [cross(hidden[:, c * out_step : (c + 1) * out_step]) for c in range(OUT_CHUNKS)]
     near_rows = jnp.concatenate(exchange(select(near_pick, hidden)), axis=0)
     far_rows = [

time: 329 us -> 329 us (level)
  Pallas kernels: 291 us -> 295 us
    pallas_call x1, Pallas kernels: 291 us -> 295 us  [fused(): pl.pallas_call(fused_kernel, in_specs=[vmem] * 4 + [hbm], out_specs=[hbm,...]
    unnamed x8 -> x6, local copies, waits for them, and re-layouts: 25.1 us -> 25.1 us
  transfers between devices with their start and end apart: 1 -> 0, of which waited for: 0 -> 0; matrix products, arithmetic and copies ran while one was open for 1% -> 0% of each run, Pallas kernels for 0% -> 0%
where the time goes in v1:
time: 329 us; the launch traced here: 326 us
  Pallas kernels  295 us (90%)
  local copies, waits for them, and re-layouts  30.6 us (9%)
    pallas_call x1, Pallas kernels, fused(): pl.pallas_call(fused_kernel, in_specs=[vmem] * 4 + [hbm], out_specs=[hbm,...  295 us
    unnamed x6, local copies, waits for them, and re-layouts  25.1 us

profile of v1, /device:TPU:1, one launch (start us, length us, event | category | flops | bytes accessed | tf_op | source)
XLA Modules:
  0.0 326.3 jit_solution(6642806424046342144)
XLA Ops:
  0.6 0.0 copy-start
  0.7 0.1 fusion
  0.8 0.8 broadcast_in_dim.18
  1.5 0.1 reshape.70
  1.6 0.6 pad.4.route
  2.2 0.0 copy-done
  2.2 0.7 gather_fusion.1
  2.9 0.1 slice_select_fusion
  3.0 0.8 copy.13
  3.8 1.8 gather_fusion
  5.6 0.1 slice.21
  5.7 0.8 copy.14
  6.4 294.7 %fused.1 = (bf16[4752,3584]{1,0:T(8,128)(2,1)}, bf16[256,3584]{1,0:T(8,128)(2,1)}) custom-call(bf16[256,3584]{1,0:T(8,128)(2,1)} %hidden.1, s32[8,256]{1,0:T(8,128)} %pad.4.route, s32[19,16,256]{2,1,0:T(8,128)} %bitcast.22, f32[19,16,256]{2,1,0:T(8,128)} %bitcast.21, bf16[4752,3584]{1,0:T(8,128)(2,1)} %weight.1), custom_call_target="tpu_custom_call" | custom-call | tf_op jit(solution)/shard_map/fused/pallas_call | solution.py:426
  301.2 0.0 copy-start.1
  301.2 23.8 %copy.17 = bf16[4752,3584]{1,0:T(8,128)(2,1)} copy(bf16[4752,3584]{1,0:T(8,128)(2,1)} %get-tuple-element.6) | data formatting | bytes 68124672
  325.1 0.0 copy-done.1
  325.1 1.2 copy.18
  (7 shorter events, 0.1 us)
Async XLA Ops:
  0.6 1.6 copy-start
  301.2 23.9 %copy-start.1 = (bf16[256,3584]{1,0:T(8,128)(2,1)S(1)}, bf16[256,3584]{1,0:T(8,128)(2,1)}, u32[]{:S(2)}) copy-start(bf16[256,3584]{1,0:T(8,128)(2,1)} %get-tuple-element.7) | copy-start | bytes 5505028
